TPU v7x, 32 devices: a whole 2x2x4 slice. The times are simulated.
32 devices in a mesh: turb: 16 (over z, x, core), snap: 2 (over y).
Axes of the slice: x: 2, y: 2, z: 4, core: 2. Of those that a mesh axis runs over, the one named last changes fastest.
Arguments:
- velocity: bfloat16 [128, 2, 128, 128], P('turb', 'snap'), may hold values from -6 to 6
- turbine_rows: int32 [128], replicated, may hold values from 0 to 127, as said below
- wake_pairs: int32 [256, 2], P('turb'), may hold values from 0 to 127, as said below
Outputs:
- pair_corr: float32 [256, 128, 128], P('turb', 'snap')
- turbine_corr: float32 [128, 2, 128, 128], P('turb', None, 'snap')
Inputs may be any that keep to these rules, and one draw needn't show every extreme that they name: `turbine_rows`: A permutation of the turbines. `wake_pairs`: the 16 pairs of each aligned block of 16 rows (those of one turbine group) name 32 different turbines. Of these, at most 2 have storage rows of any one group (rows g * 8 to (g + 1) * 8 - 1), and in every block some group has exactly 2.
All inputs are finite; a program needn't handle non-finite values.
Results may differ from a plain program's by a relative error of at most 0.0089.
Values may be sent and summed in bfloat16 or wider, within the bound.
A program may use at most 64 MiB of HBM per device.

v0:
```python
import jax
import jax.numpy as jnp
from jax import lax
from jax.sharding import PartitionSpec as P


def basis_tables(side_cells):
    ramp_index = jnp.arange(side_cells, dtype=jnp.int32)
    folded = ramp_index[:, None] * ramp_index[None, :] % side_cells
    angles = folded.astype(jnp.float32) * (2.0 * jnp.pi / side_cells)
    scale_factor = 1.0 / jnp.sqrt(jnp.float32(side_cells))
    return (jnp.cos(angles) * scale_factor, -jnp.sin(angles) * scale_factor)


def forward_planes(planes, narrow_re, narrow_im):
    lead_shape = planes.shape[:-2]
    side_cells = planes.shape[-1]
    flat_rows = planes.reshape(-1, side_cells)
    half_re = (
        jnp.dot(flat_rows, narrow_re, preferred_element_type=jnp.float32)
        .astype(jnp.bfloat16)
        .reshape(-1, side_cells, side_cells)
    )
    half_im = (
        jnp.dot(flat_rows, narrow_im, preferred_element_type=jnp.float32)
        .astype(jnp.bfloat16)
        .reshape(-1, side_cells, side_cells)
    )
    real_part = jnp.einsum(
        "ca,nab->ncb", narrow_re, half_re, preferred_element_type=jnp.float32
    ) - jnp.einsum("ca,nab->ncb", narrow_im, half_im, preferred_element_type=jnp.float32)
    imag_part = jnp.einsum(
        "ca,nab->ncb", narrow_re, half_im, preferred_element_type=jnp.float32
    ) + jnp.einsum("ca,nab->ncb", narrow_im, half_re, preferred_element_type=jnp.float32)
    stacked = jnp.stack([real_part, imag_part], axis=1).astype(jnp.bfloat16)
    return stacked.reshape(lead_shape + (2, side_cells, side_cells))


def inverse_pairs(cross_spec, wide_re, wide_im):
    highest = lax.Precision.HIGHEST
    cross_re = cross_spec[:, 0]
    cross_im = cross_spec[:, 1]
    mixed_re = jnp.einsum(
        "ca,nab->ncb", wide_re, cross_re, precision=highest, preferred_element_type=jnp.float32
    ) + jnp.einsum(
        "ca,nab->ncb", wide_im, cross_im, precision=highest, preferred_element_type=jnp.float32
    )
    mixed_im = jnp.einsum(
        "ca,nab->ncb", wide_re, cross_im, precision=highest, preferred_element_type=jnp.float32
    ) - jnp.einsum(
        "ca,nab->ncb", wide_im, cross_re, precision=highest, preferred_element_type=jnp.float32
    )
    return jnp.einsum(
        "nab,bc->nac", mixed_re, wide_re, precision=highest, preferred_element_type=jnp.float32
    ) + jnp.einsum(
        "nab,bc->nac", mixed_im, wide_im, precision=highest, preferred_element_type=jnp.float32
    )


def body(velocity, turbine_rows, wake_pairs):
    group_count = lax.axis_size("turb")
    local_turb = velocity.shape[0]
    local_snaps = velocity.shape[1]
    side_cells = velocity.shape[-1]
    local_pairs = wake_pairs.shape[0]
    capacity = max(2, 2 * local_pairs // group_count)
    slot_count = group_count * capacity
    snapshots = local_snaps * lax.axis_size("snap")
    wide_re, wide_im = basis_tables(side_cells)
    narrow_re = wide_re.astype(jnp.bfloat16)
    narrow_im = wide_im.astype(jnp.bfloat16)
    end_count = 2 * local_pairs
    end_rows = jnp.take(turbine_rows, jnp.concatenate([wake_pairs[:, 0], wake_pairs[:, 1]]), axis=0)
    end_index = jnp.arange(end_count, dtype=jnp.int32)
    source_group = end_rows // local_turb
    same_source = (source_group[:, None] == source_group[None, :]) & (
        end_index[None, :] < end_index[:, None]
    )
    slot_rank = jnp.sum(same_source.astype(jnp.int32), axis=1)
    end_slot = source_group * capacity + slot_rank
    end_code = end_rows % local_turb * 2 + (end_index >= local_pairs).astype(jnp.int32)
    slot_hits = (end_slot[None, :] == jnp.arange(slot_count, dtype=jnp.int32)[:, None]).astype(
        jnp.int32
    )
    wanted = (jnp.sum(slot_hits * (end_code + 1)[None, :], axis=1) - 1).reshape(
        group_count, capacity
    )
    slot_owner = jnp.sum(slot_hits * (end_index + 1)[None, :], axis=1) - 1
    asked_codes = lax.all_to_all(wanted, "turb", split_axis=0, concat_axis=0, tiled=True)
    asked_turb = (jnp.maximum(asked_codes, 0) // 2).reshape(-1)
    outgoing = jnp.take(velocity, asked_turb, axis=0).reshape(
        (group_count, capacity) + velocity.shape[1:]
    )
    received = forward_planes(
        lax.all_to_all(outgoing, "turb", split_axis=0, concat_axis=0, tiled=True),
        narrow_re,
        narrow_im,
    )
    received = received.reshape((slot_count,) + received.shape[2:])
    gathered = jnp.take(received, end_slot, axis=0)
    upstream = gathered[:local_pairs]
    downstream = gathered[local_pairs:]
    up_re = upstream[:, :, 0].astype(jnp.float32)
    up_im = upstream[:, :, 1].astype(jnp.float32)
    down_re = downstream[:, :, 0].astype(jnp.float32)
    down_im = downstream[:, :, 1].astype(jnp.float32)
    cross_re = jnp.sum(up_re * down_re + up_im * down_im, axis=1) / snapshots
    cross_im = jnp.sum(up_re * down_im - up_im * down_re, axis=1) / snapshots
    cross_spec = jnp.stack([cross_re, cross_im], axis=1)
    partial_terms = inverse_pairs(cross_spec, wide_re, wide_im)
    pair_corr = lax.psum_scatter(partial_terms, "snap", scatter_dimension=1, tiled=True)
    back_pairs = jnp.maximum(slot_owner, 0) % local_pairs
    outgoing_back = jnp.take(pair_corr, back_pairs, axis=0).reshape(
        (group_count, capacity) + pair_corr.shape[1:]
    )
    returned = lax.all_to_all(outgoing_back, "turb", split_axis=0, concat_axis=0, tiled=True)
    code_hits = (
        asked_codes.reshape(-1)[None, :] == jnp.arange(2 * local_turb, dtype=jnp.int32)[:, None]
    ).astype(jnp.float32)
    totals = jnp.dot(
        code_hits,
        returned.reshape(slot_count, -1),
        precision=lax.Precision.HIGHEST,
        preferred_element_type=jnp.float32,
    )
    turbine_corr = totals.reshape((local_turb, 2) + pair_corr.shape[1:])
    return (pair_corr, turbine_corr)


def solution(mesh):
    return jax.shard_map(
        body,
        mesh=mesh,
        in_specs=(P("turb", "snap", None, None), P(), P("turb", None)),
        out_specs=(P("turb", "snap", None), P("turb", None, "snap", None)),
        check_vma=False,
    )
```

profile of v0, /device:TPU:0, one launch (start us, length us, event | category | flops | bytes accessed | tf_op | source)
XLA Modules:
  0.0 134.4 jit_solution(3475938752255068279)
XLA Ops:
  7.2 0.0 copy-start
  7.2 0.8 slice_bitcast_fusion.1
  7.9 0.1 fusion.134
  8.0 1.4 %gather_fusion = s32[32]{0:T(128)S(1)} fusion(s32[128]{0:T(128)} %param.4, s32[1024]{0:T(1024)S(1)} %pad_clamp_fusion.3), kind=kCustom, calls=%fused_computation | custom fusion | bytes 384 | tf_op jit(solution)/shard_map/jit(_take)/gather | solution.py:73
  9.4 0.1 fusion.60
  9.5 0.2 convert_reduce_fusion
  9.7 0.1 select_reduce_fusion
  9.8 0.1 sub.45
  9.9 13.6 %all_to_all.19 = s32[16,1,2]{2,1,0:T(1,128)S(1)} all-to-all(s32[16,1,2]{2,1,0:T(1,128)S(1)} %bitcast.131), channel_id=1, replica_groups=mesh['turb'=16,'snap'=2] {'turb'}, dimensions={0} | all-to-all | bytes 256 | tf_op jit(solution)/shard_map/all_to_all | solution.py:89
  23.5 0.1 copy.67
  23.6 0.1 copy.70
  23.7 0.1 div.46
  23.8 0.1 copy.69
  23.9 0.1 and.210
  24.0 0.1 copy.68
  24.1 0.0 copy-done
  24.1 0.7 gather_fusion.1
  24.8 1.2 broadcast_select_fusion
  26.0 3.7 %all-to-all-start.1 = ((bf16[16,2,1,128,128]{4,3,1,2,0:T(8,128)(2,1)}), bf16[16,2,1,128,128]{4,3,1,2,0:T(8,128)(2,1)S(1)}, u32[]{:S(2)}, u32[]{:S(2)}) async-start(bf16[16,2,1,128,128]{4,3,1,2,0:T(8,128)(2,1)} %broadcast_select_fusion), calls=%async_computation.1 | async-start | bytes 2097152 | tf_op jit(solution)/shard_map/all_to_all | solution.py:95
  29.7 0.0 reduce-scatter.2.cloned.1.call-start
  29.7 0.1 fusion.58
  29.8 22.7 %all-to-all-done.1 = bf16[16,2,1,128,128]{4,3,1,2,0:T(8,128)(2,1)S(1)} async-done(((bf16[16,2,1,128,128]{4,3,1,2,0:T(8,128)(2,1)}), bf16[16,2,1,128,128]{4,3,1,2,0:T(8,128)(2,1)S(1)}, u32[]{:S(2)}, u32[]{:S(2)}) %all-to-all-start.1) | async-done | bytes 1048608 | tf_op jit(solution)/shard_map/all_to_all | solution.py:95
  52.5 0.7 convolution_convert_fusion.1
  53.2 0.7 convolution_convert_fusion
  53.9 0.7 fusion.32
  54.6 0.7 fusion.30
  55.2 0.7 fusion
  55.9 0.7 fusion.1
  56.6 1.5 %maximum_bitcast_fusion = bf16[32,2,128,128]{2,3,0,1:T(8,128)(2,1)} fusion(bf16[32,1,1,128,128]{3,4,0,2,1:T(8,128)(2,1)S(1)} %fusion.1, bf16[32,1,1,128,128]{3,4,0,2,1:T(8,128)(2,1)S(1)} %fusion), kind=kLoop, calls=%fused_computation.6 | loop fusion | flops 1048576 | bytes 4194304 | tf_op jit(solution)/shard_map/stack | solution.py:35
  58.2 2.5 %gather_fusion.2 = bf16[32,2,128,128]{2,3,1,0:T(8,128)(2,1)S(1)} fusion(bf16[32,2,128,128]{2,3,0,1:T(8,128)(2,1)} %maximum_bitcast_fusion, s32[1024]{0:T(1024)S(1)} %pad_clamp_fusion.1), kind=kCustom, calls=%fused_computation.2 | custom fusion | bytes 4194432 | tf_op jit(solution)/shard_map/jit(_take)/gather | solution.py:100
  60.7 0.3 bitcast_select_fusion
  61.0 1.4 %fusion.18 = f32[16,128,128]{2,1,0:T(8,128)S(1)} fusion(bf16[32,1,2,128,128]{3,4,2,0,1:T(8,128)(2,1)S(1)} %bitcast_select_fusion), kind=kOutput, calls=%fused_computation.42 | convolution fusion | flops 404996096 | bytes 3145728 | tf_op jit(solution)/shard_map/ca,nab->ncb/dot_general | solution.py:48
  62.4 1.4 %fusion.22 = f32[16,128,128]{2,1,0:T(8,128)S(1)} fusion(bf16[32,1,2,128,128]{3,4,2,0,1:T(8,128)(2,1)S(1)} %bitcast_select_fusion), kind=kOutput, calls=%fused_computation.46 | convolution fusion | flops 404996096 | bytes 3145728 | tf_op jit(solution)/shard_map/ca,nab->ncb/dot_general | solution.py:43
  63.8 1.4 %fusion.2 = f32[16,128,128]{1,2,0:T(8,128)S(1)} fusion(f32[16,128,128]{2,1,0:T(8,128)S(1)} %fusion.18, bf16[32,1,2,128,128]{3,4,2,0,1:T(8,128)(2,1)S(1)} %bitcast_select_fusion), kind=kOutput, calls=%fused_computation.14 | convolution fusion | flops 405274624 | bytes 4194304 | tf_op jit(solution)/shard_map/ca,nab->ncb/dot_general | solution.py:50
  65.1 1.4 %fusion.3 = f32[16,128,128]{1,2,0:T(8,128)S(1)} fusion(f32[16,128,128]{2,1,0:T(8,128)S(1)} %fusion.22, bf16[32,1,2,128,128]{3,4,2,0,1:T(8,128)(2,1)S(1)} %bitcast_select_fusion), kind=kOutput, calls=%fused_computation.16 | convolution fusion | flops 405274624 | bytes 4194304 | tf_op jit(solution)/shard_map/ca,nab->ncb/dot_general | solution.py:45
  66.5 2.1 %fusion.20 = f32[16,128,128]{2,1,0:T(8,128)S(1)} fusion(f32[16,128,128]{1,2,0:T(8,128)S(1)} %fusion.3), kind=kOutput, calls=%fused_computation.44 | convolution fusion | flops 402898944 | bytes 2097152 | tf_op jit(solution)/shard_map/nab,bc->nac/dot_general | solution.py:53
  68.7 2.9 %convolution_add_fusion = f32[16,128,128]{2,1,0:T(8,128)} fusion(f32[16,128,128]{2,1,0:T(8,128)S(1)} %fusion.20, f32[16,128,128]{1,2,0:T(8,128)S(1)} %fusion.2), kind=kOutput, calls=%fused_computation.12 | convolution fusion | flops 403177472 | bytes 3145728 | tf_op jit(solution)/shard_map/nab,bc->nac/dot_general | solution.py:55
  71.6 0.0 reduce-scatter.2.cloned.1.call-update
  71.6 0.1 rem.251
  71.7 0.1 copy.77
  71.8 0.1 copy.81
  71.9 22.3 %reduce-scatter.2.cloned.1.call-done = f32[16,64,128]{2,1,0:T(8,128)} async-done(((f32[16,128,128]{2,1,0:T(8,128)}), f32[16,64,128]{2,1,0:T(8,128)}) %reduce-scatter.2.cloned.1.call-update) | async-done | bytes 524304 | tf_op jit(solution)/shard_map/reduce_scatter | solution.py:111
  94.2 1.7 %gather_fusion.3 = f32[32,64,128]{2,1,0:T(8,128)S(1)} fusion(f32[16,64,128]{2,1,0:T(8,128)} %reduce-scatter.2.cloned.1.call-done, s32[1024]{0:T(1024)S(1)} %pad_clamp_fusion), kind=kCustom, calls=%fused_computation.3 | custom fusion | bytes 2097280 | tf_op jit(solution)/shard_map/jit(_take)/gather | solution.py:113
  95.9 1.1 broadcast_select_fusion.1
  97.0 5.6 %all-to-all-start.2 = ((f32[16,2,64,128]{3,2,1,0:T(8,128)}), f32[16,2,64,128]{3,2,1,0:T(8,128)S(1)}, u32[]{:S(2)}, u32[]{:S(2)}) async-start(f32[16,2,64,128]{3,2,1,0:T(8,128)} %broadcast_select_fusion.1), calls=%async_computation.3 | async-start | bytes 2097152 | tf_op jit(solution)/shard_map/all_to_all | solution.py:116
  102.7 0.5 broadcast.789
  103.2 0.7 reduce.3
  103.9 0.1 all_to_all.14
  104.0 21.7 %all-to-all-done.2 = f32[16,2,64,128]{3,2,1,0:T(8,128)S(1)} async-done(((f32[16,2,64,128]{3,2,1,0:T(8,128)}), f32[16,2,64,128]{3,2,1,0:T(8,128)S(1)}, u32[]{:S(2)}, u32[]{:S(2)}) %all-to-all-start.2) | async-done | bytes 1048608 | tf_op jit(solution)/shard_map/all_to_all | solution.py:116
  125.6 1.1 fusion.10
  126.7 0.9 copy.83
  (14 shorter events, 0.1 us)
Async XLA Ops:
  7.2 16.9 %copy-start = (bf16[8,1,128,128]{3,2,1,0:T(8,128)(2,1)S(1)}, bf16[8,1,128,128]{3,2,1,0:T(8,128)(2,1)}, u32[]{:S(2)}) copy-start(bf16[8,1,128,128]{3,2,1,0:T(8,128)(2,1)} %param.3) | copy-start | bytes 786436
  26.0 26.6 %all-to-all-start.1 = ((bf16[16,2,1,128,128]{4,3,1,2,0:T(8,128)(2,1)}), bf16[16,2,1,128,128]{4,3,1,2,0:T(8,128)(2,1)S(1)}, u32[]{:S(2)}, u32[]{:S(2)}) async-start(bf16[16,2,1,128,128]{4,3,1,2,0:T(8,128)(2,1)} %broadcast_select_fusion), calls=%async_computation.1 | async-start | bytes 2097152 | tf_op jit(solution)/shard_map/all_to_all | solution.py:95
  29.7 64.6 %reduce-scatter.2.cloned.1.call-start = ((), (), s32[]{:S(2)}) async-start(), calls=%async_computation.4 | async-start | bytes 1572864 | tf_op jit(solution)/shard_map/reduce_scatter | solution.py:111
  97.0 28.6 %all-to-all-start.2 = ((f32[16,2,64,128]{3,2,1,0:T(8,128)}), f32[16,2,64,128]{3,2,1,0:T(8,128)S(1)}, u32[]{:S(2)}, u32[]{:S(2)}) async-start(f32[16,2,64,128]{3,2,1,0:T(8,128)} %broadcast_select_fusion.1), calls=%async_computation.3 | async-start | bytes 2097152 | tf_op jit(solution)/shard_map/all_to_all | solution.py:116
Sparse Core Ops, SparseCore 0:
  71.7 22.4 reduce-scatter.1
where the time goes:
time: 136 us; the launch traced here: 134 us
  waiting for transfers between devices  66.7 us (49%)
  matrix products  15.7 us (12%)
  between operations  14.3 us (11%)
  blocking collectives  13.6 us (10%)
  local copies, waits for them, and re-layouts  9.43 us (7%)
  starting transfers between devices  9.32 us (7%)
  other arithmetic  5.42 us (4%)
    all_to_all x1, waiting for transfers between devices, body(): lax.all_to_all(outgoing, 'turb', split_axis=0, concat_axis=0, tiled=True)  22.7 us
    reduce_scatter x1, waiting for transfers between devices, body(): lax.psum_scatter(partial_terms, 'snap', scatter_dimension=1, tiled=True)  22.3 us
    all_to_all x1, waiting for transfers between devices, body(): lax.all_to_all(outgoing_back, 'turb', split_axis=0, concat_axis=0, tiled=...  21.7 us
    all_to_all x1, blocking collectives, body(): lax.all_to_all(wanted, 'turb', split_axis=0, concat_axis=0, tiled=True)  13.6 us
    all_to_all x1, starting transfers between devices, body(): lax.all_to_all(outgoing_back, 'turb', split_axis=0, concat_axis=0, tiled=...  5.63 us
    all_to_all x1, starting transfers between devices, body(): lax.all_to_all(outgoing, 'turb', split_axis=0, concat_axis=0, tiled=True)  3.65 us
    dot_general x1, matrix products, inverse_pairs(): jnp.einsum('nab,bc->nac', mixed_im, wide_im, precision=highest, preferred...  2.93 us
  transfers between devices with their start and end apart: 3, of which 3 were waited for; matrix products, arithmetic and copies ran while one was open for 1% of the time, Pallas kernels for 0%

commit v1 on v0

v1 whole, which is shorter than its diff:
```python
import functools

import jax
import jax.numpy as jnp
from jax import lax
from jax.experimental import pallas as pl
from jax.experimental.pallas import tpu as pltpu
from jax.sharding import PartitionSpec as P

MESH = pl.DeviceIdType.MESH
CAP = 2
BATCH = 4


def basis_tables(side):
    ramp = jnp.arange(side, dtype=jnp.int32)
    folded = ramp[:, None] * ramp[None, :] % side
    angles = folded.astype(jnp.float32) * (2.0 * jnp.pi / side)
    scale = 1.0 / jnp.sqrt(jnp.float32(side))
    return (jnp.cos(angles) * scale, -jnp.sin(angles) * scale)


def dot(a, b):
    return jnp.dot(a, b, preferred_element_type=jnp.float32)


def kernel(
    n,
    ns,
    slot_ref,
    owner_ref,
    vel,
    wanted,
    right_fwd,
    left_fwd,
    left_inv,
    right_inv,
    pair_out,
    turb_out,
    req,
    req_s,
    sendb,
    recvb,
    spec,
    part,
    ssend,
    srecv,
    bsend,
    brecv,
    local_sem,
    req_send,
    req_recv,
    fwd_send,
    fwd_recv,
    snap_send,
    snap_recv,
    back_send,
    back_recv,
):
    me = lax.axis_index("turb")
    sn = lax.axis_index("snap")
    side = vel.shape[-1]
    pairs, rows = pair_out.shape[:2]
    outs = 2 * turb_out.shape[0]
    chunks = pairs // BATCH

    def ahead(k):
        return lax.rem(me + k, n)

    def behind(k):
        return lax.rem(me + n - k, n)

    def snap_at(j):
        return lax.rem(sn + j, ns)

    def loop(lo, hi, step):
        def wrapped(i, carry):
            step(i)
            return carry

        lax.fori_loop(lo, hi, wrapped, 0)

    barrier = pltpu.get_barrier_semaphore()
    loop(1, n, lambda k: pl.semaphore_signal(barrier, inc=1, device_id={"turb": ahead(k)}, device_id_type=MESH))
    loop(1, ns, lambda j: pl.semaphore_signal(barrier, inc=1, device_id={"snap": snap_at(j)}, device_id_type=MESH))
    pl.semaphore_wait(barrier, n + ns - 2)

    def req_copy(k):
        return pltpu.make_async_remote_copy(
            wanted.at[k], req.at[k], req_send.at[k], req_recv.at[k],
            device_id={"turb": behind(k)}, device_id_type=MESH,
        )

    def fwd_copy(k):
        return pltpu.make_async_remote_copy(
            sendb.at[k], recvb.at[k], fwd_send.at[k], fwd_recv.at[k],
            device_id={"turb": ahead(k)}, device_id_type=MESH,
        )

    def snap_copy(j, c):
        span = pl.ds(c * BATCH, BATCH)
        return pltpu.make_async_remote_copy(
            ssend.at[j, span], srecv.at[j, span], snap_send.at[j, c], snap_recv.at[j, c],
            device_id={"snap": snap_at(j)}, device_id_type=MESH,
        )

    def back_copy(k):
        return pltpu.make_async_remote_copy(
            bsend.at[k], brecv.at[k], back_send.at[k], back_recv.at[k],
            device_id={"turb": behind(k)}, device_id_type=MESH,
        )

    loop(1, n, lambda k: req_copy(k).start())
    req[0] = wanted[0]
    loop(1, n, lambda k: req_copy(k).wait_recv())
    to_scalars = pltpu.make_async_copy(req, req_s, local_sem)
    to_scalars.start()
    to_scalars.wait()

    def send_planes(k):
        for c in range(CAP):
            sendb[k, c] = vel[req_s[k, 0, CAP + c]]
        fwd_copy(k).start()

    loop(1, n, send_planes)
    for c in range(CAP):
        recvb[0, c] = vel[req_s[0, 0, CAP + c]]

    def forward(k):
        planes = recvb[k].reshape(CAP * side, side)
        half = dot(planes, right_fwd[...]).astype(jnp.bfloat16)
        top = jnp.concatenate([half[:side, :side], half[side:, :side]], axis=1)
        low = jnp.concatenate([half[:side, side:], half[side:, side:]], axis=1)
        both = dot(left_fwd[...], jnp.concatenate([top, low], axis=0)).astype(jnp.bfloat16)
        spec[k * CAP] = both[:, :side]
        spec[k * CAP + 1] = both[:, side:]

    forward(0)

    def arrive(k):
        fwd_copy(k).wait_recv()
        forward(k)

    loop(1, n, arrive)

    def cross(p):
        up = spec[slot_ref[p]].astype(jnp.float32)
        down = spec[slot_ref[pairs + p]].astype(jnp.float32)
        ur, ui, dr, di = up[:side], up[side:], down[:side], down[side:]
        both = jnp.concatenate([ur * dr + ui * di, ur * di - ui * dr], axis=0)
        return (both * (1.0 / ns)).astype(jnp.bfloat16)

    def pair_chunk(c):
        for b in range(0, BATCH, 2):
            p = c * BATCH + b
            mixed = dot(left_inv[...], jnp.concatenate([cross(p), cross(p + 1)], axis=1)).astype(jnp.bfloat16)
            wide = jnp.concatenate(
                [
                    jnp.concatenate([mixed[:side, :side], mixed[side:, :side]], axis=1),
                    jnp.concatenate([mixed[:side, side:], mixed[side:, side:]], axis=1),
                ],
                axis=0,
            )
            out = dot(wide, right_inv[...])
            part[b] = out[:side]
            part[b + 1] = out[side:]
        for b in range(BATCH):
            p = c * BATCH + b
            pair_out[p] = part[b, pl.ds(pl.multiple_of(sn * rows, rows), rows)]

            def give(j):
                at = pl.multiple_of(snap_at(j) * rows, rows)
                ssend[j, p] = part[b, pl.ds(at, rows)].astype(jnp.bfloat16)

            loop(1, ns, give)
        loop(1, ns, lambda j: snap_copy(j, c).start())

    loop(0, chunks, pair_chunk)

    def collect(c):
        def one(j):
            snap_copy(j, c).wait_recv()
            for b in range(BATCH):
                p = c * BATCH + b
                pair_out[p] = pair_out[p] + srecv[j, p].astype(jnp.float32)

        loop(1, ns, one)

    loop(0, chunks, collect)

    def send_back(k):
        for c in range(CAP):
            bsend[k, c] = pair_out[owner_ref[k * CAP + c]].astype(jnp.bfloat16)
        back_copy(k).start()

    loop(1, n, send_back)
    for c in range(CAP):
        brecv[0, c] = pair_out[owner_ref[c]].astype(jnp.bfloat16)

    turb_out[...] = jnp.zeros_like(turb_out)

    def total(k):
        got = [brecv[k, c].astype(jnp.float32) for c in range(CAP)]
        codes = [req_s[k, 0, c] for c in range(CAP)]
        for o in range(outs):
            add = turb_out[o // 2, o % 2]
            for c in range(CAP):
                add = add + got[c] * jnp.where(codes[c] == o, 1.0, 0.0)
            turb_out[o // 2, o % 2] = add

    total(0)

    def returned(k):
        back_copy(k).wait_recv()
        total(k)

    loop(1, n, returned)

    def drain(k):
        req_copy(k).wait_send()
        fwd_copy(k).wait_send()
        back_copy(k).wait_send()

    loop(1, n, drain)
    loop(0, chunks, lambda c: loop(1, ns, lambda j: snap_copy(j, c).wait_send()))


def body(velocity, turbine_rows, wake_pairs):
    n = lax.axis_size("turb")
    ns = lax.axis_size("snap")
    me = lax.axis_index("turb")
    local_turb, local_snaps, side = velocity.shape[:3]
    assert local_snaps == 1
    pairs = wake_pairs.shape[0]
    slots = n * CAP
    rows = side // ns
    wide_re, wide_im = basis_tables(side)
    re, im = wide_re.astype(jnp.bfloat16), wide_im.astype(jnp.bfloat16)
    right_fwd = jnp.concatenate([re, im], axis=1)
    left_fwd = jnp.concatenate([jnp.concatenate([re, -im], 1), jnp.concatenate([im, re], 1)], 0)
    left_inv = jnp.concatenate([jnp.concatenate([re, im], 1), jnp.concatenate([-im, re], 1)], 0)
    right_inv = jnp.concatenate([re, im], axis=0)

    ends = wake_pairs.T.reshape(-1)
    turbines = jnp.arange(turbine_rows.shape[0], dtype=jnp.int32)
    end_rows = jnp.sum(jnp.where(ends[:, None] == turbines[None, :], turbine_rows[None, :], 0), axis=1)
    end_index = jnp.arange(2 * pairs, dtype=jnp.int32)
    group = end_rows // local_turb
    same = (group[:, None] == group[None, :]) & (end_index[None, :] < end_index[:, None])
    rank = jnp.sum(same.astype(jnp.int32), axis=1)
    slot = lax.rem(me + n - group, n) * CAP + rank
    code = end_rows % local_turb * 2 + (end_index >= pairs).astype(jnp.int32)
    hits = slot[None, :] == jnp.arange(slots, dtype=jnp.int32)[:, None]
    codes = jnp.sum(jnp.where(hits, code[None, :] + 1, 0), axis=1) - 1
    owner = jnp.sum(jnp.where(hits, end_index[None, :] % pairs, 0), axis=1)
    codes = codes.reshape(n, CAP)
    wanted = jnp.concatenate([codes, jnp.maximum(codes, 0) // 2], axis=1)
    wanted = jnp.pad(wanted, ((0, 0), (0, 128 - 2 * CAP)))[:, None, :]

    vmem = pl.BlockSpec(memory_space=pltpu.VMEM)
    smem = pl.BlockSpec(memory_space=pltpu.SMEM)
    chunks = pairs // BATCH
    bf16 = jnp.bfloat16
    sem = pltpu.SemaphoreType.DMA
    return pl.pallas_call(
        functools.partial(kernel, n, ns),
        out_shape=(
            jax.ShapeDtypeStruct((pairs, rows, side), jnp.float32),
            jax.ShapeDtypeStruct((local_turb, 2, rows, side), jnp.float32),
        ),
        in_specs=[smem, smem] + [vmem] * 6,
        out_specs=(vmem, vmem),
        scratch_shapes=[
            pltpu.VMEM((n, 1, 128), jnp.int32),
            pltpu.SMEM((n, 1, 128), jnp.int32),
            pltpu.VMEM((n, CAP, side, side), bf16),
            pltpu.VMEM((n, CAP, side, side), bf16),
            pltpu.VMEM((slots, 2 * side, side), bf16),
            pltpu.VMEM((BATCH, side, side), jnp.float32),
            pltpu.VMEM((ns, pairs, rows, side), bf16),
            pltpu.VMEM((ns, pairs, rows, side), bf16),
            pltpu.VMEM((n, CAP, rows, side), bf16),
            pltpu.VMEM((n, CAP, rows, side), bf16),
            sem,
            sem((n,)),
            sem((n,)),
            sem((n,)),
            sem((n,)),
            sem((ns, chunks)),
            sem((ns, chunks)),
            sem((n,)),
            sem((n,)),
        ],
        compiler_params=pltpu.CompilerParams(
            collective_id=0, has_side_effects=True, vmem_limit_bytes=48 * 2**20
        ),
    )(slot, owner, velocity[:, 0], wanted, right_fwd, left_fwd, left_inv, right_inv)


def solution(mesh):
    return jax.shard_map(
        body,
        mesh=mesh,
        in_specs=(P("turb", "snap", None, None), P(), P("turb", None)),
        out_specs=(P("turb", "snap", None), P("turb", None, "snap", None)),
        check_vma=False,
    )
```

time: 136 us -> 64.7 us (0.48); the launches traced: 134 us -> 64.5 us
  waiting for transfers between devices: 66.7 us -> 0 us
  Pallas kernels: 0 us -> 58.7 us
  matrix products: 15.7 us -> 0 us
  blocking collectives: 13.6 us -> 0 us
  between operations: 14.3 us -> 0.72 us
  starting transfers between devices: 9.32 us -> 0 us
  local copies, waits for them, and re-layouts: 9.43 us -> 3.9 us
  other arithmetic: 5.42 us -> 1.19 us
    pallas_call x0 -> x1, Pallas kernels: none -> 58.7 us  [body(): pl.pallas_call(functools.partial(kernel, n, ns), out_shape=(jax.ShapeDtyp...]
    all_to_all x2 -> x0, waiting for transfers between devices: 44.4 us -> none  [the longest x1 22.7 us: body(): lax.all_to_all(outgoing, 'turb', split_axis=0, concat_axis=0, tiled=True)]
    reduce_scatter x1 -> x0, waiting for transfers between devices: 22.3 us -> none  [body(): lax.psum_scatter(partial_terms, 'snap', scatter_dimension=1, tiled=True)]
    dot_general x13 -> x0, matrix products: 15.7 us -> none  [the longest x1 2.93 us: inverse_pairs(): jnp.einsum('nab,bc->nac', mixed_im, wide_im, precision=highest, preferred...]
    all_to_all x1 -> x0, blocking collectives: 13.6 us -> none  [body(): lax.all_to_all(wanted, 'turb', split_axis=0, concat_axis=0, tiled=True)]
    all_to_all x2 -> x0, starting transfers between devices: 9.28 us -> none  [the longest x1 5.63 us: body(): lax.all_to_all(outgoing_back, 'turb', split_axis=0, concat_axis=0, tiled=...]
    gather x4 -> x0, local copies, waits for them, and re-layouts: 6.29 us -> none  [the longest x1 2.54 us: body(): gathered = jnp.take(received, end_slot, axis=0)]
    unnamed x3 -> x8, local copies, waits for them, and re-layouts: 0.9 us -> 3.73 us
  transfers between devices with their start and end apart: 3 -> 0, of which waited for: 3 -> 0; matrix products, arithmetic and copies ran while one was open for 1% -> 0% of each run, Pallas kernels for 0% -> 0%
where the time goes in v1:
time: 64.7 us; the launch traced here: 64.5 us
  Pallas kernels  58.7 us (91%)
  local copies, waits for them, and re-layouts  3.9 us (6%)
  other arithmetic  1.19 us (2%)
  between operations  0.72 us (1%)
    pallas_call x1, Pallas kernels, body(): pl.pallas_call(functools.partial(kernel, n, ns), out_shape=(jax.ShapeDtyp...  58.7 us
    unnamed x8, local copies, waits for them, and re-layouts  3.73 us

profile of v1, /device:TPU:0, one launch (start us, length us, event | category | flops | bytes accessed | tf_op | source)
XLA Modules:
  0.0 64.5 jit_solution(13366260844415078711)
XLA Ops:
  0.6 0.0 copy-start.1
  0.6 0.7 %copy-done.1 = s32[16,2]{0,1:T(2,128)S(1)} copy-done((s32[16,2]{0,1:T(2,128)S(1)}, s32[16,2]{0,1:T(2,128)}, u32[]{:S(2)}) %copy-start.1) | copy-done | bytes 152
  1.3 0.0 copy-start.2
  1.3 0.1 eq.23
  1.4 0.6 copy-done.2
  2.0 0.2 select_reduce_fusion.2
  2.2 0.2 convert_reduce_fusion
  2.4 0.1 select_reduce_fusion
  2.5 0.1 sub.32
  2.6 0.1 pad_add_fusion
  2.7 0.3 fusion.9
  3.0 0.3 multiply_convert_fusion
  3.3 0.0 copy-start
  3.3 0.9 %copy-done = bf16[8,1,128,128]{3,2,1,0:T(8,128)(2,1)S(1)} copy-done((bf16[8,1,128,128]{3,2,1,0:T(8,128)(2,1)S(1)}, bf16[8,1,128,128]{3,2,1,0:T(8,128)(2,1)}, u32[]{:S(2)}) %copy-start) | copy-done | bytes 262168
  4.2 58.7 %shard_map.50 = (f32[16,64,128]{2,1,0:T(8,128)S(1)}, f32[8,2,64,128]{3,2,1,0:T(8,128)S(1)}) custom-call(s32[32]{0:T(128)S(1)} %get-tuple-element.9.slot_ref, s32[32]{0:T(128)S(1)} %get-tuple-element.3.owner_ref, bf16[8,128,128]{2,1,0:T(8,128)(2,1)S(1)} %bitcast.3, s32[16,1,128]{2,1,0:T(1,128)S(1)} %bitcast.4, ...), custom_call_target="tpu_custom_call" | custom-call | tf_op jit(solution)/shard_map/pallas_call | solution.py:265
  62.9 0.8 %copy.10 = f32[16,64,128]{2,1,0:T(8,128)} copy(f32[16,64,128]{2,1,0:T(8,128)S(1)} %get-tuple-element.14) | data formatting | bytes 1048576
  63.7 0.8 %copy.11 = f32[8,2,64,128]{3,2,1,0:T(8,128)} copy(f32[8,2,64,128]{3,2,1,0:T(8,128)S(1)} %get-tuple-element.15) | data formatting | bytes 1048576
  (8 shorter events, 0.1 us)
Async XLA Ops:
  0.6 0.7 %copy-start.1 = (s32[16,2]{0,1:T(2,128)S(1)}, s32[16,2]{0,1:T(2,128)}, u32[]{:S(2)}) copy-start(s32[16,2]{0,1:T(2,128)} %param.5) | copy-start | bytes 388
  1.3 0.7 %copy-start.2 = (s32[128]{0:T(128)S(1)}, s32[128]{0:T(128)}, u32[]{:S(2)}) copy-start(s32[128]{0:T(128)} %param.4) | copy-start | bytes 1540
  3.3 1.0 %copy-start = (bf16[8,1,128,128]{3,2,1,0:T(8,128)(2,1)S(1)}, bf16[8,1,128,128]{3,2,1,0:T(8,128)(2,1)}, u32[]{:S(2)}) copy-start(bf16[8,1,128,128]{3,2,1,0:T(8,128)(2,1)} %param.3) | copy-start | bytes 786436

commit v2 on v1

v2 whole, which is shorter than its diff:
```python
import functools

import jax
import jax.numpy as jnp
import ml_dtypes
import numpy as np
from jax import lax
from jax.experimental import pallas as pl
from jax.experimental.pallas import tpu as pltpu
from jax.sharding import PartitionSpec as P

MESH = pl.DeviceIdType.MESH
CAP = 2
BATCH = 4
CUTS = 4


def basis_tables(side):
    ramp = np.arange(side, dtype=np.int32)
    angles = (ramp[:, None] * ramp[None, :] % side) * (2.0 * np.pi / side)
    return (
        (np.cos(angles) / np.sqrt(side)).astype(np.float32),
        (-np.sin(angles) / np.sqrt(side)).astype(np.float32),
    )


def dot(a, b):
    return jnp.dot(a, b, preferred_element_type=jnp.float32)


def tables(n, me, local_turb, turb_rows, wake):
    pairs = wake.shape[0]
    count = 2 * pairs
    shift = local_turb.bit_length() - 1
    total = turb_rows.shape[1]
    ends = jnp.concatenate([wake[:, 0:1], wake[:, 1:2]], axis=0)
    lanes = lax.broadcasted_iota(jnp.int32, (count, total), 1)
    rows_col = jnp.sum(jnp.where(ends == lanes, turb_rows[...], 0), axis=1, keepdims=True)
    down = lax.broadcasted_iota(jnp.int32, (count, count), 0)
    over = lax.broadcasted_iota(jnp.int32, (count, count), 1)
    rows_row = jnp.sum(jnp.where(down == over, rows_col, 0), axis=0, keepdims=True)
    group_col = lax.shift_right_logical(rows_col, jnp.full_like(rows_col, shift))
    group_row = lax.shift_right_logical(rows_row, jnp.full_like(rows_row, shift))
    same = (group_col == group_row) & (down < over)
    rank = jnp.sum(jnp.where(same, 1, 0), axis=0, keepdims=True)
    back = me - group_row
    slot = jnp.where(back < 0, back + n, back) * CAP + rank
    end = lax.broadcasted_iota(jnp.int32, (1, count), 1)
    code = (rows_row - group_row * local_turb) * 2 + jnp.where(end >= pairs, 1, 0)
    pair = jnp.where(end >= pairs, end - pairs, end)
    place = lax.broadcasted_iota(jnp.int32, (n, count), 0)
    lane = lax.broadcasted_iota(jnp.int32, (n, 128), 1)
    table = jnp.zeros((n, 128), jnp.int32)
    for c in range(CAP):
        hit = slot == place * CAP + c
        codes = jnp.sum(jnp.where(hit, code + 1, 0), axis=1, keepdims=True) - 1
        owner = jnp.sum(jnp.where(hit, pair, 0), axis=1, keepdims=True)
        plane = lax.shift_right_logical(jnp.maximum(codes, 0), jnp.ones_like(codes))
        table = jnp.where(lane == c, codes, table)
        table = jnp.where(lane == CAP + c, plane, table)
        table = jnp.where(lane == 2 * CAP + c, owner, table)
    last = jnp.concatenate([jnp.minimum(slot, n * CAP - 1), jnp.zeros((1, 128 - count), jnp.int32)], axis=1)
    return jnp.concatenate([table, last], axis=0)


def kernel(
    n,
    ns,
    vel_hbm,
    turb_rows,
    wake,
    right_fwd_hbm,
    left_fwd_hbm,
    left_inv_hbm,
    right_inv_hbm,
    pair_out,
    turb_out,
    vel,
    right_fwd,
    left_fwd,
    left_inv,
    right_inv,
    wanted,
    own_s,
    req,
    req_s,
    sendb,
    recvb,
    spec,
    part,
    ssend,
    srecv,
    bsend,
    brecv,
    load_sem,
    own_sem,
    local_sem,
    req_send,
    req_recv,
    fwd_send,
    fwd_recv,
    snap_send,
    snap_recv,
    back_send,
    back_recv,
):
    me = lax.axis_index("turb")
    sn = lax.axis_index("snap")
    side = vel.shape[-1]
    pairs, rows = pair_out.shape[:2]
    outs = 2 * turb_out.shape[0]
    chunks = pairs // BATCH
    cuts, tall = bsend.shape[1], bsend.shape[3]

    def ahead(k):
        return lax.rem(me + k, n)

    def behind(k):
        return lax.rem(me + n - k, n)

    def snap_at(j):
        return lax.rem(sn + j, ns)

    def loop(lo, hi, step):
        def wrapped(i, carry):
            step(i)
            return carry

        lax.fori_loop(lo, hi, wrapped, 0)

    loads = [
        pltpu.make_async_copy(a, b, load_sem.at[i])
        for i, (a, b) in enumerate(
            [
                (vel_hbm, vel),
                (right_fwd_hbm, right_fwd),
                (left_fwd_hbm, left_fwd),
                (left_inv_hbm, left_inv),
                (right_inv_hbm, right_inv),
            ]
        )
    ]
    barrier = pltpu.get_barrier_semaphore()
    loop(1, n, lambda k: pl.semaphore_signal(barrier, inc=1, device_id={"turb": ahead(k)}, device_id_type=MESH))
    loop(1, ns, lambda j: pl.semaphore_signal(barrier, inc=1, device_id={"snap": snap_at(j)}, device_id_type=MESH))
    for load in loads:
        load.start()
    wanted[...] = tables(n, me, turb_out.shape[0], turb_rows, wake)[:, None, :]
    own = pltpu.make_async_copy(wanted, own_s, own_sem)
    own.start()
    pl.semaphore_wait(barrier, n + ns - 2)

    def req_copy(k):
        return pltpu.make_async_remote_copy(
            wanted.at[k], req.at[k], req_send.at[k], req_recv.at[k],
            device_id={"turb": behind(k)}, device_id_type=MESH,
        )

    def fwd_copy(k):
        return pltpu.make_async_remote_copy(
            sendb.at[k], recvb.at[k], fwd_send.at[k], fwd_recv.at[k],
            device_id={"turb": ahead(k)}, device_id_type=MESH,
        )

    def snap_copy(j, r):
        return pltpu.make_async_remote_copy(
            ssend.at[j, r], srecv.at[j, r], snap_send.at[j, r], snap_recv.at[j, r],
            device_id={"snap": snap_at(j)}, device_id_type=MESH,
        )

    def back_copy(k, r):
        return pltpu.make_async_remote_copy(
            bsend.at[k, r], brecv.at[k, r], back_send.at[k, r], back_recv.at[k, r],
            device_id={"turb": behind(k)}, device_id_type=MESH,
        )

    loop(1, n, lambda k: req_copy(k).start())
    req[0] = wanted[0]
    loop(1, n, lambda k: req_copy(k).wait_recv())
    to_scalars = pltpu.make_async_copy(req, req_s, local_sem)
    to_scalars.start()
    to_scalars.wait()
    own.wait()
    for load in loads:
        load.wait()

    def send_planes(k):
        for c in range(CAP):
            sendb[k, c] = vel[req_s[k, 0, CAP + c]]
        fwd_copy(k).start()

    loop(1, n, send_planes)
    for c in range(CAP):
        recvb[0, c] = vel[req_s[0, 0, CAP + c]]

    def forward(k):
        planes = recvb[k].reshape(CAP * side, side)
        half = dot(planes, right_fwd[...]).astype(jnp.bfloat16)
        top = jnp.concatenate([half[:side, :side], half[side:, :side]], axis=1)
        low = jnp.concatenate([half[:side, side:], half[side:, side:]], axis=1)
        both = dot(left_fwd[...], jnp.concatenate([top, low], axis=0)).astype(jnp.bfloat16)
        spec[k * CAP] = both[:, :side]
        spec[k * CAP + 1] = both[:, side:]

    forward(0)

    def arrive(k):
        fwd_copy(k).wait_recv()
        forward(k)

    loop(1, n, arrive)

    def cross(p):
        up = spec[own_s[n, 0, p]].astype(jnp.float32)
        down = spec[own_s[n, 0, pairs + p]].astype(jnp.float32)
        ur, ui, dr, di = up[:side], up[side:], down[:side], down[side:]
        both = jnp.concatenate([ur * dr + ui * di, ur * di - ui * dr], axis=0)
        return (both * (1.0 / ns)).astype(jnp.bfloat16)

    def pair_chunk(c):
        for b in range(0, BATCH, 2):
            p = c * BATCH + b
            mixed = dot(left_inv[...], jnp.concatenate([cross(p), cross(p + 1)], axis=1)).astype(jnp.bfloat16)
            wide = jnp.concatenate(
                [
                    jnp.concatenate([mixed[:side, :side], mixed[side:, :side]], axis=1),
                    jnp.concatenate([mixed[:side, side:], mixed[side:, side:]], axis=1),
                ],
                axis=0,
            )
            out = dot(wide, right_inv[...])
            part[b] = out[:side]
            part[b + 1] = out[side:]
        for b in range(BATCH):
            p = c * BATCH + b
            pair_out[p] = part[b, pl.ds(pl.multiple_of(sn * rows, rows), rows)]

            def give(j):
                for r in range(cuts):
                    at = pl.multiple_of(snap_at(j) * rows, rows) + r * tall
                    ssend[j, r, p] = part[b, pl.ds(at, tall)].astype(jnp.bfloat16)

            loop(1, ns, give)

    loop(0, chunks, pair_chunk)
    for r in range(cuts):
        loop(1, ns, lambda j: snap_copy(j, r).start())

    for r in range(cuts):
        span = pl.ds(r * tall, tall)

        def collect(j):
            snap_copy(j, r).wait_recv()
            pair_out[:, span] = pair_out[:, span] + srecv[j, r].astype(jnp.float32)

        loop(1, ns, collect)

        def send_back(k):
            for c in range(CAP):
                bsend[k, r, c] = pair_out[own_s[k, 0, 2 * CAP + c], span].astype(jnp.bfloat16)
            back_copy(k, r).start()

        loop(1, n, send_back)
        for c in range(CAP):
            brecv[0, r, c] = pair_out[own_s[0, 0, 2 * CAP + c], span].astype(jnp.bfloat16)

    turb_out[...] = jnp.zeros_like(turb_out)
    for r in range(cuts):
        span = pl.ds(r * tall, tall)

        def total(k):
            got = [brecv[k, r, c].astype(jnp.float32) for c in range(CAP)]
            codes = [req_s[k, 0, c] for c in range(CAP)]
            for o in range(outs):
                add = turb_out[o // 2, o % 2, span]
                for c in range(CAP):
                    add = add + got[c] * jnp.where(codes[c] == o, 1.0, 0.0)
                turb_out[o // 2, o % 2, span] = add

        total(0)

        def returned(k):
            back_copy(k, r).wait_recv()
            total(k)

        loop(1, n, returned)

    def drain(k):
        req_copy(k).wait_send()
        fwd_copy(k).wait_send()
        for r in range(cuts):
            back_copy(k, r).wait_send()

    loop(1, n, drain)
    for r in range(cuts):
        loop(1, ns, lambda j: snap_copy(j, r).wait_send())


def body(velocity, turbine_rows, wake_pairs):
    n = lax.axis_size("turb")
    ns = lax.axis_size("snap")
    local_turb, local_snaps, side = velocity.shape[:3]
    assert local_snaps == 1
    pairs = wake_pairs.shape[0]
    slots = n * CAP
    rows = side // ns
    cuts = max(1, min(CUTS, rows // 16))
    assert local_turb & (local_turb - 1) == 0 and 2 * pairs <= 128
    wide_re, wide_im = basis_tables(side)
    re, im = wide_re.astype(ml_dtypes.bfloat16), wide_im.astype(ml_dtypes.bfloat16)
    right_fwd = np.concatenate([re, im], axis=1)
    left_fwd = np.block([[re, -im], [im, re]])
    left_inv = np.block([[re, im], [-im, re]])
    right_inv = np.concatenate([re, im], axis=0)
    basis = [jnp.asarray(a) for a in (right_fwd, left_fwd, left_inv, right_inv)]

    vmem = pl.BlockSpec(memory_space=pltpu.VMEM)
    hbm = pl.BlockSpec(memory_space=pl.ANY)
    bf16 = jnp.bfloat16
    sem = pltpu.SemaphoreType.DMA
    return pl.pallas_call(
        functools.partial(kernel, n, ns),
        out_shape=(
            jax.ShapeDtypeStruct((pairs, rows, side), jnp.float32),
            jax.ShapeDtypeStruct((local_turb, 2, rows, side), jnp.float32),
        ),
        in_specs=[hbm, vmem, vmem] + [hbm] * 4,
        out_specs=(vmem, vmem),
        scratch_shapes=[
            pltpu.VMEM((local_turb, side, side), bf16),
            *[pltpu.VMEM(a.shape, bf16) for a in basis],
            pltpu.VMEM((n + 1, 1, 128), jnp.int32),
            pltpu.SMEM((n + 1, 1, 128), jnp.int32),
            pltpu.VMEM((n, 1, 128), jnp.int32),
            pltpu.SMEM((n, 1, 128), jnp.int32),
            pltpu.VMEM((n, CAP, side, side), bf16),
            pltpu.VMEM((n, CAP, side, side), bf16),
            pltpu.VMEM((slots, 2 * side, side), bf16),
            pltpu.VMEM((BATCH, side, side), jnp.float32),
            pltpu.VMEM((ns, cuts, pairs, rows // cuts, side), bf16),
            pltpu.VMEM((ns, cuts, pairs, rows // cuts, side), bf16),
            pltpu.VMEM((n, cuts, CAP, rows // cuts, side), bf16),
            pltpu.VMEM((n, cuts, CAP, rows // cuts, side), bf16),
            sem((5,)),
            sem,
            sem,
            sem((n,)),
            sem((n,)),
            sem((n,)),
            sem((n,)),
            sem((ns, cuts)),
            sem((ns, cuts)),
            sem((n, cuts)),
            sem((n, cuts)),
        ],
        compiler_params=pltpu.CompilerParams(
            collective_id=0, has_side_effects=True, vmem_limit_bytes=48 * 2**20
        ),
    )(velocity[:, 0], turbine_rows[None, :], wake_pairs, *basis)


def solution(mesh):
    return jax.shard_map(
        body,
        mesh=mesh,
        in_specs=(P("turb", "snap", None, None), P(), P("turb", None)),
        out_specs=(P("turb", "snap", None), P("turb", None, "snap", None)),
        check_vma=False,
    )
```

time: 64.7 us -> 65.4 us (1.011)
  local copies, waits for them, and re-layouts: 3.9 us -> 7.35 us
  Pallas kernels: 58.7 us -> 57.1 us
  other arithmetic: 1.19 us -> 0 us
    unnamed x8 -> x17, local copies, waits for them, and re-layouts: 3.73 us -> 7.35 us
    pallas_call x1, Pallas kernels: 58.7 us -> 57.1 us  [body(): pl.pallas_call(functools.partial(kernel, n, ns), out_shape=(jax.ShapeDtyp...]
where the time goes in v2:
time: 65.4 us; the launch traced here: 65.1 us
  Pallas kernels  57.1 us (87%)
  local copies, waits for them, and re-layouts  7.35 us (11%)
    pallas_call x1, Pallas kernels, body(): pl.pallas_call(functools.partial(kernel, n, ns), out_shape=(jax.ShapeDtyp...  57.1 us
    unnamed x17, local copies, waits for them, and re-layouts  7.35 us

profile of v2, /device:TPU:0, one launch (start us, length us, event | category | flops | bytes accessed | tf_op | source)
XLA Modules:
  0.0 65.1 jit_solution(6703926718708813576)
XLA Ops:
  0.6 0.0 copy-start.6
  0.6 0.7 %copy-done.6 = s32[16,2]{0,1:T(2,128)S(1)} copy-done((s32[16,2]{0,1:T(2,128)S(1)}, s32[16,2]{0,1:T(2,128)}, u32[]{:S(2)}) %copy-start.6) | copy-done | bytes 152
  1.3 0.0 copy-start.5
  1.3 0.1 copy.9.wake
  1.4 0.6 copy-done.5
  2.0 0.0 copy-start
  2.0 0.9 %copy-done = bf16[8,1,128,128]{3,2,1,0:T(8,128)(2,1)S(1)} copy-done((bf16[8,1,128,128]{3,2,1,0:T(8,128)(2,1)S(1)}, bf16[8,1,128,128]{3,2,1,0:T(8,128)(2,1)}, u32[]{:S(2)}) %copy-start) | copy-done | bytes 262168
  2.9 0.0 copy-start.1
  2.9 0.9 %copy-done.1 = bf16[256,256]{1,0:T(8,128)(2,1)S(1)} copy-done((bf16[256,256]{1,0:T(8,128)(2,1)S(1)}, bf16[256,256]{1,0:T(8,128)(2,1)}, u32[]{:S(2)}) %copy-start.1) | copy-done | bytes 131096
  3.8 0.0 copy-start.2
  3.8 0.9 %copy-done.2 = bf16[256,256]{1,0:T(8,128)(2,1)S(1)} copy-done((bf16[256,256]{1,0:T(8,128)(2,1)S(1)}, bf16[256,256]{1,0:T(8,128)(2,1)}, u32[]{:S(2)}) %copy-start.2) | copy-done | bytes 131096
  4.7 0.0 copy-start.3
  4.7 0.8 %copy-done.3 = bf16[256,128]{1,0:T(8,128)(2,1)S(1)} copy-done((bf16[256,128]{1,0:T(8,128)(2,1)S(1)}, bf16[256,128]{1,0:T(8,128)(2,1)}, u32[]{:S(2)}) %copy-start.3) | copy-done | bytes 65560
  5.6 0.0 copy-start.4
  5.6 0.8 %copy-done.4 = bf16[128,256]{1,0:T(8,128)(2,1)S(1)} copy-done((bf16[128,256]{1,0:T(8,128)(2,1)S(1)}, bf16[128,256]{1,0:T(8,128)(2,1)}, u32[]{:S(2)}) %copy-start.4) | copy-done | bytes 65560
  6.4 57.1 %shard_map.86 = (f32[16,64,128]{2,1,0:T(8,128)S(1)}, f32[8,2,64,128]{3,2,1,0:T(8,128)S(1)}) custom-call(bf16[8,128,128]{2,1,0:T(8,128)(2,1)S(1)} %bitcast.2, s32[1,128]{1,0:T(1,128)S(1)} %bitcast.3, s32[16,2]{1,0:T(8,128)S(1)} %copy.9.wake, bf16[128,256]{1,0:T(8,128)(2,1)S(1)} %copy-done.4, bf16[256,256]{1,0:T(8,128)(2,1)S(1)} %copy-done.2, ...), custom_call_target="tpu_custom_call" | custom-call | tf_op jit(solution)/shard_map/pallas_call | solution.py:321
  63.5 0.8 %copy.12 = f32[16,64,128]{2,1,0:T(8,128)} copy(f32[16,64,128]{2,1,0:T(8,128)S(1)} %get-tuple-element.4) | data formatting | bytes 1048576
  64.3 0.8 %copy.13 = f32[8,2,64,128]{3,2,1,0:T(8,128)} copy(f32[8,2,64,128]{3,2,1,0:T(8,128)S(1)} %get-tuple-element.5) | data formatting | bytes 1048576
Async XLA Ops:
  0.6 0.7 %copy-start.6 = (s32[16,2]{0,1:T(2,128)S(1)}, s32[16,2]{0,1:T(2,128)}, u32[]{:S(2)}) copy-start(s32[16,2]{0,1:T(2,128)} %param.9) | copy-start | bytes 388
  1.3 0.7 %copy-start.5 = (s32[128]{0:T(128)S(1)}, s32[128]{0:T(128)}, u32[]{:S(2)}) copy-start(s32[128]{0:T(128)} %param.8) | copy-start | bytes 1540
  2.0 0.9 %copy-start = (bf16[8,1,128,128]{3,2,1,0:T(8,128)(2,1)S(1)}, bf16[8,1,128,128]{3,2,1,0:T(8,128)(2,1)}, u32[]{:S(2)}) copy-start(bf16[8,1,128,128]{3,2,1,0:T(8,128)(2,1)} %param.7) | copy-start | bytes 786436
  2.9 0.9 %copy-start.1 = (bf16[256,256]{1,0:T(8,128)(2,1)S(1)}, bf16[256,256]{1,0:T(8,128)(2,1)}, u32[]{:S(2)}) copy-start(bf16[256,256]{1,0:T(8,128)(2,1)} %constant.10.clone.left_inv_hbm) | copy-start | bytes 393220
  3.8 0.9 %copy-start.2 = (bf16[256,256]{1,0:T(8,128)(2,1)S(1)}, bf16[256,256]{1,0:T(8,128)(2,1)}, u32[]{:S(2)}) copy-start(bf16[256,256]{1,0:T(8,128)(2,1)} %constant.9.clone.left_fwd_hbm) | copy-start | bytes 393220
  4.7 0.8 %copy-start.3 = (bf16[256,128]{1,0:T(8,128)(2,1)S(1)}, bf16[256,128]{1,0:T(8,128)(2,1)}, u32[]{:S(2)}) copy-start(bf16[256,128]{1,0:T(8,128)(2,1)} %constant.11.clone.right_inv_hbm) | copy-start | bytes 196612
  5.6 0.8 %copy-start.4 = (bf16[128,256]{1,0:T(8,128)(2,1)S(1)}, bf16[128,256]{1,0:T(8,128)(2,1)}, u32[]{:S(2)}) copy-start(bf16[128,256]{1,0:T(8,128)(2,1)} %constant.8.clone.right_fwd_hbm) | copy-start | bytes 196612

commit v3 on v2

--- a/solution.py
+++ b/solution.py
@@ -12,7 +12,7 @@
 MESH = pl.DeviceIdType.MESH
 CAP = 2
 BATCH = 4
-CUTS = 4
+CUTS = 2
 
 
 def basis_tables(side):
@@ -29,11 +29,15 @@
 
 
 def tables(n, me, local_turb, turb_rows, wake):
-    pairs = wake.shape[0]
+    pairs = wake.shape[1]
     count = 2 * pairs
     shift = local_turb.bit_length() - 1
     total = turb_rows.shape[1]
-    ends = jnp.concatenate([wake[:, 0:1], wake[:, 1:2]], axis=0)
+    first = lax.broadcasted_iota(jnp.int32, (pairs, pairs), 0)
+    second = lax.broadcasted_iota(jnp.int32, (pairs, pairs), 1)
+    ends = jnp.concatenate(
+        [jnp.sum(jnp.where(first == second, wake[i : i + 1], 0), axis=1, keepdims=True) for i in range(2)], axis=0
+    )
     lanes = lax.broadcasted_iota(jnp.int32, (count, total), 1)
     rows_col = jnp.sum(jnp.where(ends == lanes, turb_rows[...], 0), axis=1, keepdims=True)
     down = lax.broadcasted_iota(jnp.int32, (count, count), 0)
@@ -67,14 +71,16 @@
     n,
     ns,
     vel_hbm,
-    turb_rows,
-    wake,
+    turb_rows_hbm,
+    wake_hbm,
     right_fwd_hbm,
     left_fwd_hbm,
     left_inv_hbm,
     right_inv_hbm,
     pair_out,
     turb_out,
+    turb_rows,
+    wake,
     vel,
     right_fwd,
     left_fwd,
@@ -121,6 +127,14 @@
     def snap_at(j):
         return lax.rem(sn + j, ns)
 
+    def others(step):
+        def wrapped(i, carry):
+            d = (i + 1) // 2
+            step(n // 2 + d * (2 * (i % 2) - 1))
+            return carry
+
+        lax.fori_loop(0, n - 1, wrapped, 0)
+
     def loop(lo, hi, step):
         def wrapped(i, carry):
             step(i)
@@ -132,6 +146,8 @@
         pltpu.make_async_copy(a, b, load_sem.at[i])
         for i, (a, b) in enumerate(
             [
+                (turb_rows_hbm, turb_rows),
+                (wake_hbm, wake),
                 (vel_hbm, vel),
                 (right_fwd_hbm, right_fwd),
                 (left_fwd_hbm, left_fwd),
@@ -140,11 +156,13 @@
             ]
         )
     ]
+    for load in loads:
+        load.start()
     barrier = pltpu.get_barrier_semaphore()
     loop(1, n, lambda k: pl.semaphore_signal(barrier, inc=1, device_id={"turb": ahead(k)}, device_id_type=MESH))
     loop(1, ns, lambda j: pl.semaphore_signal(barrier, inc=1, device_id={"snap": snap_at(j)}, device_id_type=MESH))
-    for load in loads:
-        load.start()
+    for load in loads[:2]:
+        load.wait()
     wanted[...] = tables(n, me, turb_out.shape[0], turb_rows, wake)[:, None, :]
     own = pltpu.make_async_copy(wanted, own_s, own_sem)
     own.start()
@@ -174,14 +192,14 @@
             device_id={"turb": behind(k)}, device_id_type=MESH,
         )
 
-    loop(1, n, lambda k: req_copy(k).start())
+    others(lambda k: req_copy(k).start())
     req[0] = wanted[0]
     loop(1, n, lambda k: req_copy(k).wait_recv())
     to_scalars = pltpu.make_async_copy(req, req_s, local_sem)
     to_scalars.start()
     to_scalars.wait()
     own.wait()
-    for load in loads:
+    for load in loads[2:]:
         load.wait()
 
     def send_planes(k):
@@ -189,7 +207,7 @@
             sendb[k, c] = vel[req_s[k, 0, CAP + c]]
         fwd_copy(k).start()
 
-    loop(1, n, send_planes)
+    others(send_planes)
     for c in range(CAP):
         recvb[0, c] = vel[req_s[0, 0, CAP + c]]
 
@@ -208,7 +226,7 @@
         fwd_copy(k).wait_recv()
         forward(k)
 
-    loop(1, n, arrive)
+    others(arrive)
 
     def cross(p):
         up = spec[own_s[n, 0, p]].astype(jnp.float32)
@@ -260,7 +278,7 @@
                 bsend[k, r, c] = pair_out[own_s[k, 0, 2 * CAP + c], span].astype(jnp.bfloat16)
             back_copy(k, r).start()
 
-        loop(1, n, send_back)
+        others(send_back)
         for c in range(CAP):
             brecv[0, r, c] = pair_out[own_s[0, 0, 2 * CAP + c], span].astype(jnp.bfloat16)
 
@@ -283,7 +301,7 @@
             back_copy(k, r).wait_recv()
             total(k)
 
-        loop(1, n, returned)
+        others(returned)
 
     def drain(k):
         req_copy(k).wait_send()
@@ -294,6 +312,17 @@
     loop(1, n, drain)
     for r in range(cuts):
         loop(1, ns, lambda j: snap_copy(j, r).wait_send())
+
+
+def write_out(pairs_in, turbs_in, pairs_out, turbs_out, sems):
+    copies = [
+        pltpu.make_async_copy(pairs_in, pairs_out, sems.at[0]),
+        pltpu.make_async_copy(turbs_in, turbs_out, sems.at[1]),
+    ]
+    for copy in copies:
+        copy.start()
+    for copy in copies:
+        copy.wait()
 
 
 def body(velocity, turbine_rows, wake_pairs):
@@ -302,6 +331,7 @@
     local_turb, local_snaps, side = velocity.shape[:3]
     assert local_snaps == 1
     pairs = wake_pairs.shape[0]
+    total = turbine_rows.shape[0]
     slots = n * CAP
     rows = side // ns
     cuts = max(1, min(CUTS, rows // 16))
@@ -315,18 +345,20 @@
     basis = [jnp.asarray(a) for a in (right_fwd, left_fwd, left_inv, right_inv)]
 
     vmem = pl.BlockSpec(memory_space=pltpu.VMEM)
-    hbm = pl.BlockSpec(memory_space=pl.ANY)
+    hbm = pl.BlockSpec(memory_space=pltpu.HBM)
     bf16 = jnp.bfloat16
     sem = pltpu.SemaphoreType.DMA
-    return pl.pallas_call(
+    made = pl.pallas_call(
         functools.partial(kernel, n, ns),
         out_shape=(
             jax.ShapeDtypeStruct((pairs, rows, side), jnp.float32),
             jax.ShapeDtypeStruct((local_turb, 2, rows, side), jnp.float32),
         ),
-        in_specs=[hbm, vmem, vmem] + [hbm] * 4,
+        in_specs=[hbm] * 7,
         out_specs=(vmem, vmem),
         scratch_shapes=[
+            pltpu.VMEM((1, total), jnp.int32),
+            pltpu.VMEM((2, pairs), jnp.int32),
             pltpu.VMEM((local_turb, side, side), bf16),
             *[pltpu.VMEM(a.shape, bf16) for a in basis],
             pltpu.VMEM((n + 1, 1, 128), jnp.int32),
@@ -341,7 +373,7 @@
             pltpu.VMEM((ns, cuts, pairs, rows // cuts, side), bf16),
             pltpu.VMEM((n, cuts, CAP, rows // cuts, side), bf16),
             pltpu.VMEM((n, cuts, CAP, rows // cuts, side), bf16),
-            sem((5,)),
+            sem((7,)),
             sem,
             sem,
             sem((n,)),
@@ -354,9 +386,16 @@
             sem((n, cuts)),
         ],
         compiler_params=pltpu.CompilerParams(
-            collective_id=0, has_side_effects=True, vmem_limit_bytes=48 * 2**20
+            collective_id=0, has_side_effects=True, vmem_limit_bytes=62 * 2**20
         ),
-    )(velocity[:, 0], turbine_rows[None, :], wake_pairs, *basis)
+    )(velocity[:, 0], turbine_rows[None, :], wake_pairs.T, *basis)
+    return pl.pallas_call(
+        write_out,
+        out_shape=tuple(jax.ShapeDtypeStruct(a.shape, a.dtype) for a in made),
+        in_specs=[vmem] * 2,
+        out_specs=(hbm, hbm),
+        scratch_shapes=[sem((2,))],
+    )(*made)
 
 
 def solution(mesh):

time: 65.4 us -> 60.2 us (0.920)
  local copies, waits for them, and re-layouts: 7.35 us -> 0 us
  Pallas kernels: 57.1 us -> 59.4 us
    unnamed x17 -> x0, local copies, waits for them, and re-layouts: 7.35 us -> none
    pallas_call x0 -> x1, Pallas kernels: none -> 2.18 us  [body(): pl.pallas_call(write_out, out_shape=tuple((jax.ShapeDtypeStruct(a.shape,...]
where the time goes in v3:
time: 60.2 us; the launch traced here: 60 us
  Pallas kernels  59.4 us (99%)
  between operations  0.64 us (1%)
    pallas_call x1, Pallas kernels, body(): pl.pallas_call(functools.partial(kernel, n, ns), out_shape=(jax.ShapeDtyp...  57.2 us
    pallas_call x1, Pallas kernels, body(): pl.pallas_call(write_out, out_shape=tuple((jax.ShapeDtypeStruct(a.shape,...  2.18 us

profile of v3, /device:TPU:0, one launch (start us, length us, event | category | flops | bytes accessed | tf_op | source)
XLA Modules:
  0.0 60.0 jit_solution(2671748085839236167)
XLA Ops:
  0.6 57.2 %shard_map.86 = (f32[16,64,128]{2,1,0:T(8,128)}, f32[8,2,64,128]{3,2,1,0:T(8,128)}) custom-call(bf16[8,128,128]{2,1,0:T(8,128)(2,1)} %bitcast.3, s32[1,128]{1,0:T(1,128)} %bitcast.5, s32[2,16]{1,0:T(2,128)} %bitcast.4, bf16[128,256]{1,0:T(8,128)(2,1)} %constant.8.clone.right_fwd_hbm, bf16[256,256]{1,0:T(8,128)(2,1)} %constant.9.clone.left_fwd_hbm, ...), custom_call_target="tpu_custom_call" | custom-call | tf_op jit(solution)/shard_map/pallas_call | solution.py:351
  57.8 2.2 %shard_map.87 = (f32[16,64,128]{2,1,0:T(8,128)}, f32[8,2,64,128]{3,2,1,0:T(8,128)}) custom-call(f32[16,64,128]{2,1,0:T(8,128)} %get-tuple-element.4.pairs_in, f32[8,2,64,128]{3,2,1,0:T(8,128)} %get-tuple-element.5.turbs_in), custom_call_target="tpu_custom_call" | custom-call | tf_op jit(solution)/shard_map/pallas_call | solution.py:392

commit v4 on v3

--- a/solution.py
+++ b/solution.py
@@ -11,7 +11,7 @@
 
 MESH = pl.DeviceIdType.MESH
 CAP = 2
-BATCH = 4
+BATCH = 16
 CUTS = 2
 
 

time: 60.2 us -> 58.8 us (0.977)
  Pallas kernels: 59.4 us -> 58 us
    pallas_call x1, Pallas kernels: 57.2 us -> 55.8 us  [body(): pl.pallas_call(functools.partial(kernel, n, ns), out_shape=(jax.ShapeDtyp...]
where the time goes in v4:
time: 58.8 us; the launch traced here: 58.7 us
  Pallas kernels  58 us (99%)
  between operations  0.64 us (1%)
    pallas_call x1, Pallas kernels, body(): pl.pallas_call(functools.partial(kernel, n, ns), out_shape=(jax.ShapeDtyp...  55.8 us
    pallas_call x1, Pallas kernels, body(): pl.pallas_call(write_out, out_shape=tuple((jax.ShapeDtypeStruct(a.shape,...  2.18 us

profile of v4, /device:TPU:0, one launch (start us, length us, event | category | flops | bytes accessed | tf_op | source)
XLA Modules:
  0.0 58.7 jit_solution(517891442053282335)
XLA Ops:
  0.6 55.8 %shard_map.86 = (f32[16,64,128]{2,1,0:T(8,128)}, f32[8,2,64,128]{3,2,1,0:T(8,128)}) custom-call(bf16[8,128,128]{2,1,0:T(8,128)(2,1)} %bitcast.3, s32[1,128]{1,0:T(1,128)} %bitcast.5, s32[2,16]{1,0:T(2,128)} %bitcast.4, bf16[128,256]{1,0:T(8,128)(2,1)} %constant.8.clone.right_fwd_hbm, bf16[256,256]{1,0:T(8,128)(2,1)} %constant.9.clone.left_fwd_hbm, ...), custom_call_target="tpu_custom_call" | custom-call | tf_op jit(solution)/shard_map/pallas_call | solution.py:351
  56.5 2.2 %shard_map.87 = (f32[16,64,128]{2,1,0:T(8,128)}, f32[8,2,64,128]{3,2,1,0:T(8,128)}) custom-call(f32[16,64,128]{2,1,0:T(8,128)} %get-tuple-element.4.pairs_in, f32[8,2,64,128]{3,2,1,0:T(8,128)} %get-tuple-element.5.turbs_in), custom_call_target="tpu_custom_call" | custom-call | tf_op jit(solution)/shard_map/pallas_call | solution.py:392

commit v5 on v4

--- a/solution.py
+++ b/solution.py
@@ -12,7 +12,7 @@
 MESH = pl.DeviceIdType.MESH
 CAP = 2
 BATCH = 16
-CUTS = 2
+CUTS = 4
 
 
 def basis_tables(side):

time: 58.8 us -> 58.9 us (level)
  no operation moved by 1% of the time
where the time goes in v5:
time: 58.9 us; the launch traced here: 58.7 us
  Pallas kernels  58.1 us (99%)
  between operations  0.64 us (1%)
    pallas_call x1, Pallas kernels, body(): pl.pallas_call(functools.partial(kernel, n, ns), out_shape=(jax.ShapeDtyp...  55.9 us
    pallas_call x1, Pallas kernels, body(): pl.pallas_call(write_out, out_shape=tuple((jax.ShapeDtypeStruct(a.shape,...  2.18 us

profile of v5, /device:TPU:0, one launch (start us, length us, event | category | flops | bytes accessed | tf_op | source)
XLA Modules:
  0.0 58.7 jit_solution(14620737217340747551)
XLA Ops:
  0.6 55.9 %shard_map.86 = (f32[16,64,128]{2,1,0:T(8,128)}, f32[8,2,64,128]{3,2,1,0:T(8,128)}) custom-call(bf16[8,128,128]{2,1,0:T(8,128)(2,1)} %bitcast.3, s32[1,128]{1,0:T(1,128)} %bitcast.5, s32[2,16]{1,0:T(2,128)} %bitcast.4, bf16[128,256]{1,0:T(8,128)(2,1)} %constant.8.clone.right_fwd_hbm, bf16[256,256]{1,0:T(8,128)(2,1)} %constant.9.clone.left_fwd_hbm, ...), custom_call_target="tpu_custom_call" | custom-call | tf_op jit(solution)/shard_map/pallas_call | solution.py:351
  56.5 2.2 %shard_map.87 = (f32[16,64,128]{2,1,0:T(8,128)}, f32[8,2,64,128]{3,2,1,0:T(8,128)}) custom-call(f32[16,64,128]{2,1,0:T(8,128)} %get-tuple-element.4.pairs_in, f32[8,2,64,128]{3,2,1,0:T(8,128)} %get-tuple-element.5.turbs_in), custom_call_target="tpu_custom_call" | custom-call | tf_op jit(solution)/shard_map/pallas_call | solution.py:392
